TPU v7x, 32 devices: a whole 2x2x4 slice. The times are simulated.
32 devices in a mesh: groups: 2 (over y), row: 4 (over x, core), col: 4 (over z).
Axes of the slice: x: 2, y: 2, z: 4, core: 2. Of those that a mesh axis runs over, the one named last changes fastest.
Arguments:
- features: float32 [32, 65536], P(None, ('groups', 'row', 'col')), parts along dimension 1, may hold values from -6 to 6
- noise: float32 [65536], P(('groups', 'row', 'col')), parts along dimension 0, may hold values from 0.5 to 4
- solution: float32 [16, 65536], P(None, ('groups', 'row', 'col')), parts along dimension 1, may hold values from -6 to 6
- residual: float32 [16, 65536], P(None, ('groups', 'row', 'col')), parts along dimension 1, may hold values from -12 to 12
- direction: float32 [16, 65536], P(None, ('groups', 'row', 'col')), parts along dimension 1, may hold values from -12 to 12
- tile_rows: int32 [8, 4, 64], P(('groups', 'row'), 'col'), parts along dimension 0, may hold values from 0 to 15, as said below
- tile_cols: int32 [8, 4, 64], P(('groups', 'row'), 'col'), parts along dimension 0, may hold values from 0 to 15, as said below
- tile_count: int32 [8, 4], P(('groups', 'row'), 'col'), parts along dimension 0, may hold values from 1 to 64, as said below
Outputs:
- solution_next: float32 [16, 65536], P(None, ('groups', 'row', 'col')), parts along dimension 1
- residual_next: float32 [16, 65536], P(None, ('groups', 'row', 'col')), parts along dimension 1
- direction_next: float32 [16, 65536], P(None, ('groups', 'row', 'col')), parts along dimension 1
There are 2 independent parts, one for each index of `groups`. A program takes and returns all parts, laid end to end along the dimension named above; each array names one. Nothing has to cross between parts.
Inputs may be any that keep to these rules, and one draw needn't show every extreme that they name: `tile_rows`: every listed slot names a tile with I <= J; the slots of one device name distinct tiles. `tile_cols`: see tile_rows. `tile_count`: some device of every problem lists 64 tiles.
All inputs are finite; a program needn't handle non-finite values.
Results may differ from a plain program's by a relative error of at most 0.0003.
Values sent between devices are 32-bit elements; how exact they have to be, the bound alone decides.
A program may use at most 64 MiB of HBM per device.

v0:
```python
import math
import jax
import jax.numpy as jnp
from jax import lax
from jax.sharding import PartitionSpec as P

BLK_DEV = 4
HIGH = lax.Precision.HIGHEST


def tile_kernel(row_points, col_points):
    inner = lax.dot_general(
        row_points,
        col_points,
        (((0,), (0,)), ((), ())),
        precision=HIGH,
        preferred_element_type=jnp.float32,
    )
    row_norms = jnp.sum(row_points * row_points, 0)
    col_norms = jnp.sum(col_points * col_points, 0)
    dist_sq = jnp.maximum(row_norms[:, None] + col_norms[None, :] - 2.0 * inner, 0.0)
    radius = jnp.sqrt(dist_sq) / (1.5 * math.sqrt(row_points.shape[0]))
    inside = jnp.maximum(1.0 - radius, 0.0)
    return inside**4 * (4.0 * radius + 1.0)


def gram(left, right):
    return lax.dot_general(
        left, right, (((1,), (1,)), ((), ())), precision=HIGH, preferred_element_type=jnp.float32
    )


def symmetric(matrix):
    return 0.5 * (matrix + matrix.T)


def spd_solve(matrix, target):
    lower = jnp.linalg.cholesky(matrix)
    half_way = lax.linalg.triangular_solve(lower, target, left_side=True, lower=True)
    return lax.linalg.triangular_solve(
        lower, half_way, left_side=True, lower=True, transpose_a=True
    )


def apply_left(coeffs, field):
    return lax.dot_general(
        coeffs, field, (((0,), (0,)), ((), ())), precision=HIGH, preferred_element_type=jnp.float32
    )


def add_at(running, addend, start):
    axis_last = running.ndim - 1
    current = lax.dynamic_slice_in_dim(running, start, addend.shape[-1], axis_last)
    return lax.dynamic_update_slice_in_dim(running, current + addend, start, axis_last)


def reduce_rows(row_image, row_degree):
    return (
        lax.psum_scatter(row_image, "col", scatter_dimension=1, tiled=True),
        lax.psum_scatter(row_degree, "col", scatter_dimension=0, tiled=True),
    )


def reduce_cols(col_image, col_degree):
    return (
        lax.psum_scatter(col_image, "row", scatter_dimension=1, tiled=True),
        lax.psum_scatter(col_degree, "row", scatter_dimension=0, tiled=True),
    )


def on_device(features, noise, solution, residual, direction, tile_rows, tile_cols, tile_count):
    block_width = features.shape[1] // BLK_DEV
    row_slots = tile_rows[0, 0]
    col_slots = tile_cols[0, 0]
    tile_total = tile_count[0, 0]
    rank_row = lax.axis_index("row")
    rank_col = lax.axis_index("col")
    span = lax.axis_size("col") * BLK_DEV
    row_feat, row_dir = (
        lax.all_gather(features, "col", axis=1, tiled=True),
        lax.all_gather(direction, "col", axis=1, tiled=True),
    )
    col_feat, col_dir = (
        lax.all_gather(features, "row", axis=1, tiled=True),
        lax.all_gather(direction, "row", axis=1, tiled=True),
    )
    side_count = direction.shape[0]
    initial = (
        jnp.zeros((side_count, row_feat.shape[1]), jnp.float32),
        jnp.zeros((row_feat.shape[1],), jnp.float32),
        jnp.zeros((side_count, col_feat.shape[1]), jnp.float32),
        jnp.zeros((col_feat.shape[1],), jnp.float32),
    )

    def one_tile(tile_slot, carried):
        to_row, deg_row, to_col, deg_col = carried
        local_i = row_slots[tile_slot]
        local_j = col_slots[tile_slot]
        start_i = local_i * block_width
        start_j = local_j * block_width
        used_flag = (tile_slot < tile_total).astype(jnp.float32)
        kernel = (
            tile_kernel(
                lax.dynamic_slice_in_dim(row_feat, start_i, block_width, 1),
                lax.dynamic_slice_in_dim(col_feat, start_j, block_width, 1),
            )
            * used_flag
        )
        dir_cols = lax.dynamic_slice_in_dim(col_dir, start_j, block_width, 1)
        row_term = lax.dot_general(
            dir_cols,
            kernel,
            (((1,), (1,)), ((), ())),
            precision=HIGH,
            preferred_element_type=jnp.float32,
        )
        to_row = add_at(to_row, row_term, start_i)
        deg_row = add_at(deg_row, jnp.sum(kernel, 1), start_i)
        big_i = rank_row * span + local_i
        big_j = local_j // BLK_DEV * span + rank_col * BLK_DEV + local_j % BLK_DEV
        mirror = (big_i != big_j).astype(jnp.float32)
        dir_rows = lax.dynamic_slice_in_dim(row_dir, start_i, block_width, 1)
        col_term = (
            lax.dot_general(
                dir_rows,
                kernel,
                (((1,), (0,)), ((), ())),
                precision=HIGH,
                preferred_element_type=jnp.float32,
            )
            * mirror
        )
        to_col = add_at(to_col, col_term, start_j)
        deg_col = add_at(deg_col, jnp.sum(kernel, 0) * mirror, start_j)
        return (to_row, deg_row, to_col, deg_col)

    def one_turn(turn_index, carried):
        for inner_step in range(4):
            carried = one_tile(turn_index * 4 + inner_step, carried)
        return carried

    carried = lax.fori_loop(0, row_slots.shape[0] // 4, one_turn, initial)
    row_image, row_degree = reduce_rows(carried[0], carried[1])
    col_image, col_degree = reduce_cols(carried[2], carried[3])
    degree = row_degree + col_degree
    image = (noise + degree)[None, :] * direction + row_image + col_image
    curv_sum, norm_sum = lax.psum(
        (gram(direction, image), gram(residual, residual)), ("row", "col")
    )
    curvature = symmetric(curv_sum)
    norms_now = symmetric(norm_sum)
    alpha = spd_solve(curvature, norms_now)
    residual_next = residual - apply_left(alpha, image)
    norms_next = symmetric(lax.psum(gram(residual_next, residual_next), ("row", "col")))
    solution_next = solution + apply_left(alpha, direction)
    beta = spd_solve(norms_now, norms_next)
    direction_next = residual_next + apply_left(beta, direction)
    return (solution_next, residual_next, direction_next)


def solution(mesh):
    in_specs = (
        P(None, ("groups", "row", "col")),
        P(("groups", "row", "col")),
        P(None, ("groups", "row", "col")),
        P(None, ("groups", "row", "col")),
        P(None, ("groups", "row", "col")),
        P(("groups", "row"), "col", None),
        P(("groups", "row"), "col", None),
        P(("groups", "row"), "col"),
    )
    out_specs = (
        P(None, ("groups", "row", "col")),
        P(None, ("groups", "row", "col")),
        P(None, ("groups", "row", "col")),
    )
    return jax.shard_map(
        on_device, mesh=mesh, in_specs=in_specs, out_specs=out_specs, check_vma=False
    )
```

profile of v0, /device:TPU:0, one launch (start us, length us, event | category | flops | bytes accessed | tf_op | source)
XLA Modules:
  0.0 874.8 jit_solution(3112990234694962577)
XLA Ops:
  8.8 20.4 %all_gather.15 = f32[16,8192]{1,0:T(8,128)S(1)} all-gather(f32[16,2048]{1,0:T(8,128)S(1)} %copy-done), channel_id=1, replica_groups=mesh['groups'=2,'row'=4,'col'=4] {'col'}, dimensions={1}, use_global_device_ids=true | all-gather | bytes 655360 | tf_op jit(solution)/shard_map/all_gather | solution.py:81
  29.2 7.2 all_gather.12
  36.4 6.0 all-gather.3.cloned.1.call-done
  42.4 17.7 %all-gather.5.cloned.1.call-done = f32[32,8192]{1,0:T(8,128)} async-done(((f32[32,2048]{1,0:T(8,128)}), f32[32,8192]{1,0:T(8,128)}) %all-gather.5.cloned.1.call-update) | async-done | bytes 1048592 | tf_op jit(solution)/shard_map/all_gather | solution.py:84
  60.9 658.1 %while.22 = (s32[]{:T(128)}, f32[16,8192]{1,0:T(8,128)S(1)}, f32[8192]{0:T(1024)S(1)}, f32[16,8192]{1,0:T(8,128)S(1)}, f32[8192]{0:T(1024)S(1)}, /*index=5*/s32[...) while((s32[]{:T(128)}, f32[16,8192]{1,0:T(8,128)S(1)}, ...), condition=%wide.region_17.18_spmd, body=%wide.region_0.17_spmd.sunk | while | flops 821393472 | bytes 14518369 | solution.py:142
  88.2 2.7 fusion.150
  129.4 2.7 fusion.150
  170.5 2.7 fusion.150
  211.6 2.7 fusion.150
  252.8 2.7 fusion.150
  293.9 2.7 fusion.150
  335.0 2.7 fusion.150
  376.2 2.7 fusion.150
  417.3 2.7 fusion.150
  458.4 2.7 fusion.150
  540.7 2.7 fusion.150
  581.8 2.7 fusion.150
  622.9 2.7 fusion.150
  664.0 2.7 fusion.150
  723.8 10.9 %all-reduce.1 = f32[8192]{0:T(1024)S(1)} all-reduce(f32[8192]{0:T(1024)S(1)} %get-tuple-element.410), channel_id=3, replica_groups=mesh['groups'=2,'row'=4,'col'=4] {'row'}, use_global_device_ids=true, to_apply=%region_19.20.clone | all-reduce | flops 8192 | bytes 65536
  734.7 19.5 %all-reduce = f32[8192]{0:T(1024)S(1)} all-reduce(f32[8192]{0:T(1024)S(1)} %get-tuple-element.409), channel_id=2, replica_groups=mesh['groups'=2,'row'=4,'col'=4] {'col'}, use_global_device_ids=true, to_apply=%region_18.19.clone | all-reduce | flops 8192 | bytes 65536
  754.3 9.7 %reduce-scatter.5.cloned.1.call-done = f32[16,2048]{1,0:T(8,128)} async-done(((f32[16,8192]{1,0:T(8,128)}), f32[16,2048]{1,0:T(8,128)}) %reduce-scatter.5.cloned.1.call-update) | async-done | bytes 131088 | tf_op jit(solution)/shard_map/reduce_scatter | solution.py:66
  765.3 60.8 %all-reduce.2 = (f32[16,16]{1,0:T(8,128)S(1)}, f32[16,16]{1,0:T(8,128)S(1)}) all-reduce(f32[16,16]{1,0:T(8,128)S(1)} %fusion.77, f32[16,16]{1,0:T(8,128)S(1)} %convolution_bitcast_fusion), channel_id=1, replica_groups=mesh['groups'=2,'row'=4,'col'=4] {'row','col'}, use_global_device_ids=true, to_apply=%region_25.27 | all-reduce | flops 512 | bytes 4096 | tf_op jit(solution)/shard_map/psum | solution.py:147
  831.3 30.5 %psum.23 = f32[16,16]{1,0:T(8,128)S(1)} all-reduce(f32[16,16]{1,0:T(8,128)S(1)} %fusion.78), channel_id=1, replica_groups=mesh['groups'=2,'row'=4,'col'=4] {'row','col'}, use_global_device_ids=true, to_apply=%region_26.30 | all-reduce | flops 256 | bytes 2048 | tf_op jit(solution)/shard_map/psum | solution.py:154
  (426 shorter events, 313.2 us)
Async XLA Ops:
  7.2 35.2 %all-gather.3.cloned.1.call-start = ((), (), s32[]{:S(2)}) async-start(), calls=%async_computation.2 | async-start | bytes 1310720 | tf_op jit(solution)/shard_map/all_gather | solution.py:80
  7.9 0.9 copy-start
  7.9 52.2 %all-gather.5.cloned.1.call-start = ((), (), s32[]{:S(2)}) async-start(), calls=%async_computation.3 | async-start | bytes 1310720 | tf_op jit(solution)/shard_map/all_gather | solution.py:84
  8.7 745.7 %reduce-scatter.3.cloned.1.call-start = ((), (), s32[]{:S(2)}) async-start(), calls=%async_computation.4 | async-start | bytes 655360 | tf_op jit(solution)/shard_map/reduce_scatter | solution.py:59
  42.4 17.9 %copy-start.4 = (f32[32,8192]{1,0:T(8,128)S(1)}, f32[32,8192]{1,0:T(8,128)}, u32[]{:S(2)}) copy-start(f32[32,8192]{1,0:T(8,128)} %all-gather.3.cloned.1.call-done) | copy-start | bytes 3145732
  60.2 0.7 copy-start.8
  60.2 0.7 copy-start.9
  719.0 0.8 copy-start.2
  719.0 1.0 copy-start.1
  719.8 44.2 %reduce-scatter.5.cloned.1.call-start = ((), (), s32[]{:S(2)}) async-start(), calls=%async_computation.5 | async-start | bytes 655360 | tf_op jit(solution)/shard_map/reduce_scatter | solution.py:66
  719.9 3.7 copy-start.5
  720.4 0.7 copy-start.13
  721.1 0.7 copy-start.12
  734.7 19.6 %copy-start.11 = (f32[2048]{0:T(1024)S(1)}, f32[2048]{0:T(1024)}, u32[]{:S(2)}) copy-start(f32[2048]{0:T(1024)} %param.16) | copy-start | bytes 24580
  764.0 66.7 %copy-start.7 = (f32[16,2048]{1,0:T(8,128)S(1)}, f32[16,2048]{1,0:T(8,128)}, u32[]{:S(2)}) copy-start(f32[16,2048]{1,0:T(8,128)} %reduce-scatter.5.cloned.1.call-done) | copy-start | bytes 393220
  765.3 65.5 %copy-start.6 = (f32[16,2048]{1,0:T(8,128)S(1)}, f32[16,2048]{1,0:T(8,128)}, u32[]{:S(2)}) copy-start(f32[16,2048]{1,0:T(8,128)} %reduce-scatter.3.cloned.1.call-done) | copy-start | bytes 393220
  831.1 35.2 %copy-start.3 = (f32[16,2048]{1,0:T(8,128)}, f32[16,2048]{1,0:T(8,128)S(1)}, u32[]{:S(2)}) copy-start(f32[16,2048]{1,0:T(8,128)S(1)} %convolution_subtract_fusion) | copy-start | bytes 393220
  866.3 1.0 copy-start.10
Sparse Core Ops, SparseCore 0:
  9.6 32.7 all-gather.2
  44.0 16.1 all-gather.4
  719.9 21.7 reduce-scatter.2
  744.1 19.8 reduce-scatter.4
where the time goes:
time: 883 us; the launch traced here: 875 us
  loops' own time  326 us (37%)
  matrix products  276 us (31%)
  blocking collectives  149 us (17%)
  other arithmetic  46.4 us (5%)
  waiting for transfers between devices  35.3 us (4%)
  local copies, waits for them, and re-layouts  25.9 us (3%)
  between operations  15.3 us (2%)
    another operation x1, loops' own time, on_device(): carried = lax.fori_loop(0, row_slots.shape[0] // 4, one_turn, initial)  326 us
    dot_general x64, matrix products, tile_kernel(): lax.dot_general(row_points, col_points, (((0,), (0,)), ((), ())), precisi...  170 us
    dot_general x64, matrix products, one_tile(): lax.dot_general(dir_cols, kernel, (((1,), (1,)), ((), ())), precision=HIG...  61.8 us
    psum x1, blocking collectives, on_device(): lax.psum((gram(direction, image), gram(residual, residual)), ('row', 'col'))  60.8 us
    dot_general x64, matrix products, one_tile(): lax.dot_general(dir_rows, kernel, (((1,), (0,)), ((), ())), precision=HIG...  39.9 us
    psum x1, blocking collectives, on_device(): lax.psum(gram(residual_next, residual_next), ('row', 'col'))  30.5 us
    unnamed x2, blocking collectives  30.4 us
    dynamic_update_slice x128, other arithmetic, add_at(): lax.dynamic_update_slice_in_dim(running, current + addend, start, axis_last)  21.8 us
  transfers between devices with their start and end apart: 4, of which 3 were waited for; matrix products, arithmetic and copies ran while one was open for 0% of the time, Pallas kernels for 0%

commit v1 on v0

--- a/solution.py
+++ b/solution.py
@@ -1,3 +1,4 @@
+import functools
 import math
 import jax
 import jax.numpy as jnp
@@ -6,6 +7,40 @@
 
 BLK_DEV = 4
 HIGH = lax.Precision.HIGHEST
+
+
+def extend_islands_all(local_block, d_out):
+    local_block = jnp.moveaxis(local_block, 0, d_out)
+    built = local_block.shape
+    state_now = local_block.reshape(
+        *built[:d_out], built[d_out] * built[d_out + 1], *built[d_out + 2 :]
+    )
+    return state_now
+
+
+def create_the_signs(in_array, bus_axis):
+    wide_out = lax.axis_size(bus_axis)
+    front = lax.axis_index(bus_axis)
+    current_value, mid_arr = (wide_out, front)
+    placed, y = (in_array[None], 1)
+    while y < current_value:
+        passed = tuple(((i, i ^ y) for i in range(current_value)))
+        u1 = lax.ppermute(placed, bus_axis, perm=passed)
+        side_arr = mid_arr & y == 0
+        answer = jnp.where(side_arr, placed, u1)
+        t1 = jnp.where(side_arr, u1, placed)
+        placed = jnp.concatenate([answer, t1])
+        y *= 2
+    return placed
+
+
+def pass_tracks(mine, vals, dim_i):
+    after = create_the_signs(mine, vals)
+    left_arr = extend_islands_all(after, dim_i)
+    return left_arr
+
+
+entries_end = functools.partial(pass_tracks, vals="row", dim_i=1)
 
 
 def tile_kernel(row_points, col_points):
@@ -81,7 +116,7 @@
         lax.all_gather(direction, "col", axis=1, tiled=True),
     )
     col_feat, col_dir = (
-        lax.all_gather(features, "row", axis=1, tiled=True),
+        entries_end(features),
         lax.all_gather(direction, "row", axis=1, tiled=True),
     )
     side_count = direction.shape[0]

time: 883 us -> 867 us (0.982)
  waiting for transfers between devices: 35.3 us -> 16 us
    all_gather x1 -> x0, waiting for transfers between devices: 17.7 us -> none  [on_device(): lax.all_gather(features, 'row', axis=1, tiled=True)]
  transfers between devices with their start and end apart: 4 -> 5, of which waited for: 3 -> 3; matrix products, arithmetic and copies ran while one was open for 0% -> 0% of each run, Pallas kernels for 0% -> 0%
where the time goes in v1:
time: 867 us; the launch traced here: 858 us
  loops' own time  326 us (38%)
  matrix products  276 us (32%)
  blocking collectives  148 us (17%)
  other arithmetic  46.6 us (5%)
  local copies, waits for them, and re-layouts  25.9 us (3%)
  waiting for transfers between devices  16 us (2%)
  between operations  15.3 us (2%)
    another operation x1, loops' own time, on_device(): carried = lax.fori_loop(0, row_slots.shape[0] // 4, one_turn, initial)  326 us
    dot_general x64, matrix products, tile_kernel(): lax.dot_general(row_points, col_points, (((0,), (0,)), ((), ())), precisi...  170 us
    dot_general x64, matrix products, one_tile(): lax.dot_general(dir_cols, kernel, (((1,), (1,)), ((), ())), precision=HIG...  61.8 us
    psum x1, blocking collectives, on_device(): lax.psum((gram(direction, image), gram(residual, residual)), ('row', 'col'))  60.8 us
    dot_general x64, matrix products, one_tile(): lax.dot_general(dir_rows, kernel, (((1,), (0,)), ((), ())), precision=HIG...  39.9 us
    psum x1, blocking collectives, on_device(): lax.psum(gram(residual_next, residual_next), ('row', 'col'))  30.5 us
    unnamed x2, blocking collectives  29.6 us
    dynamic_update_slice x128, other arithmetic, add_at(): lax.dynamic_update_slice_in_dim(running, current + addend, start, axis_last)  21.8 us
  transfers between devices with their start and end apart: 5, of which 3 were waited for; matrix products, arithmetic and copies ran while one was open for 0% of the time, Pallas kernels for 0%

profile of v1, /device:TPU:0, one launch (start us, length us, event | category | flops | bytes accessed | tf_op | source)
XLA Modules:
  0.0 857.9 jit_solution(7014350370492927009)
XLA Ops:
  9.2 2.9 collective-permute-start.1
  12.1 20.8 %all_gather.11 = f32[16,8192]{1,0:T(8,128)S(1)} all-gather(f32[16,2048]{1,0:T(8,128)S(1)} %copy-done), channel_id=1, replica_groups=mesh['groups'=2,'row'=4,'col'=4] {'col'}, dimensions={1}, use_global_device_ids=true | all-gather | bytes 655360 | tf_op jit(solution)/shard_map/all_gather | solution.py:116
  32.9 6.5 all_gather.9
  39.6 4.2 all-gather.2.cloned.1.call-done
  44.5 657.9 %while.22 = (s32[]{:T(128)}, f32[16,8192]{1,0:T(8,128)S(1)}, f32[8192]{0:T(1024)S(1)}, f32[16,8192]{1,0:T(8,128)S(1)}, f32[8192]{0:T(1024)S(1)}, /*index=5*/s32[...) while((s32[]{:T(128)}, f32[16,8192]{1,0:T(8,128)S(1)}, ...), condition=%wide.region_17.18_spmd, body=%wide.region_0.17_spmd.sunk | while | flops 821393472 | bytes 14518369 | solution.py:177
  71.9 2.7 fusion.150
  113.0 2.7 fusion.150
  117.6 2.7 fusion.152
  154.2 2.7 fusion.150
  195.3 2.7 fusion.150
  231.8 2.7 fusion.148
  236.4 2.7 fusion.150
  359.7 2.7 fusion.150
  400.9 2.7 fusion.150
  442.0 2.7 fusion.150
  483.1 2.7 fusion.150
  565.3 2.7 fusion.150
  606.4 2.7 fusion.150
  647.5 2.7 fusion.150
  707.5 12.1 %all-reduce.1 = f32[8192]{0:T(1024)S(1)} all-reduce(f32[8192]{0:T(1024)S(1)} %get-tuple-element.410), channel_id=3, replica_groups=mesh['groups'=2,'row'=4,'col'=4] {'row'}, use_global_device_ids=true, to_apply=%region_19.20.clone | all-reduce | flops 8192 | bytes 65536
  719.6 17.5 %all-reduce = f32[8192]{0:T(1024)S(1)} all-reduce(f32[8192]{0:T(1024)S(1)} %get-tuple-element.409), channel_id=2, replica_groups=mesh['groups'=2,'row'=4,'col'=4] {'col'}, use_global_device_ids=true, to_apply=%region_18.19.clone | all-reduce | flops 8192 | bytes 65536
  737.1 9.9 %reduce-scatter.5.cloned.1.call-done = f32[16,2048]{1,0:T(8,128)} async-done(((f32[16,8192]{1,0:T(8,128)}), f32[16,2048]{1,0:T(8,128)}) %reduce-scatter.5.cloned.1.call-update) | async-done | bytes 131088 | tf_op jit(solution)/shard_map/reduce_scatter | solution.py:101
  748.3 60.8 %all-reduce.2 = (f32[16,16]{1,0:T(8,128)S(1)}, f32[16,16]{1,0:T(8,128)S(1)}) all-reduce(f32[16,16]{1,0:T(8,128)S(1)} %fusion.77, f32[16,16]{1,0:T(8,128)S(1)} %convolution_bitcast_fusion), channel_id=1, replica_groups=mesh['groups'=2,'row'=4,'col'=4] {'row','col'}, use_global_device_ids=true, to_apply=%region_25.27 | all-reduce | flops 512 | bytes 4096 | tf_op jit(solution)/shard_map/psum | solution.py:182
  814.4 30.5 %psum.23 = f32[16,16]{1,0:T(8,128)S(1)} all-reduce(f32[16,16]{1,0:T(8,128)S(1)} %fusion.78), channel_id=1, replica_groups=mesh['groups'=2,'row'=4,'col'=4] {'row','col'}, use_global_device_ids=true, to_apply=%region_26.30 | all-reduce | flops 256 | bytes 2048 | tf_op jit(solution)/shard_map/psum | solution.py:189
  (432 shorter events, 313.8 us)
Async XLA Ops:
  7.2 1.9 copy-start.5
  7.2 36.7 %all-gather.2.cloned.1.call-start = ((), (), s32[]{:S(2)}) async-start(), calls=%async_computation.2 | async-start | bytes 1310720 | tf_op jit(solution)/shard_map/all_gather | solution.py:115
  7.2 1.9 collective-permute-start
  7.9 729.2 %reduce-scatter.3.cloned.1.call-start = ((), (), s32[]{:S(2)}) async-start(), calls=%async_computation.3 | async-start | bytes 655360 | tf_op jit(solution)/shard_map/reduce_scatter | solution.py:94
  9.2 3.0 copy-start
  9.2 30.2 %collective-permute-start.1 = (f32[2,32,2048]{2,1,0:T(8,128)S(1)}, f32[2,32,2048]{2,1,0:T(8,128)S(1)}, u32[]{:S(2)}, u32[]{:S(2)}) collective-permute-start(f32[2,32,2048]{2,1,0:T(8,128)S(1)} %pad_maximum_fusion), channel_id=1, source_target_pairs={{0,8},{4,12},{8,0},{12,4},{1,9},{5,13},{9,1},{13,5},{2,10},{6,14},... | collective-permute-start | bytes 1572872 | tf_op jit(solution)/shard_map/ppermute | solution.py:28
  43.9 0.7 copy-start.8
  43.9 0.7 copy-start.9
  702.4 0.8 copy-start.2
  702.5 1.0 copy-start.1
  703.3 43.8 %reduce-scatter.5.cloned.1.call-start = ((), (), s32[]{:S(2)}) async-start(), calls=%async_computation.4 | async-start | bytes 655360 | tf_op jit(solution)/shard_map/reduce_scatter | solution.py:101
  703.3 3.9 copy-start.4
  704.0 0.7 copy-start.13
  704.7 0.7 copy-start.12
  719.6 17.5 %copy-start.11 = (f32[2048]{0:T(1024)S(1)}, f32[2048]{0:T(1024)}, u32[]{:S(2)}) copy-start(f32[2048]{0:T(1024)} %param.16) | copy-start | bytes 24580
  747.1 66.7 %copy-start.7 = (f32[16,2048]{1,0:T(8,128)S(1)}, f32[16,2048]{1,0:T(8,128)}, u32[]{:S(2)}) copy-start(f32[16,2048]{1,0:T(8,128)} %reduce-scatter.5.cloned.1.call-done) | copy-start | bytes 393220
  748.3 65.5 %copy-start.6 = (f32[16,2048]{1,0:T(8,128)S(1)}, f32[16,2048]{1,0:T(8,128)}, u32[]{:S(2)}) copy-start(f32[16,2048]{1,0:T(8,128)} %reduce-scatter.3.cloned.1.call-done) | copy-start | bytes 393220
  814.2 35.2 %copy-start.3 = (f32[16,2048]{1,0:T(8,128)}, f32[16,2048]{1,0:T(8,128)S(1)}, u32[]{:S(2)}) copy-start(f32[16,2048]{1,0:T(8,128)S(1)} %convolution_subtract_fusion) | copy-start | bytes 393220
  849.4 1.0 copy-start.10
Sparse Core Ops, SparseCore 0:
  9.6 34.2 all-gather.1
  703.4 21.1 reduce-scatter.2
  727.0 19.9 reduce-scatter.4
